TPU v7x, 512 devices: a whole 4x8x8 slice. The times are simulated.
512 devices in a mesh: gal: 64 (over x, z, core), pix: 8 (over y).
Axes of the slice: x: 4, y: 8, z: 8, core: 2. Of those that a mesh axis runs over, the one named last changes fastest.
Arguments:
- spectra: bfloat16 [32768, 8192], P('gal', 'pix'), may hold values from -500 to 500
- sketch: bfloat16 [32768, 128], P('gal'), may hold values from -0.25 to 0.25
- block_mask: int32 [64, 64], P('gal', 'pix'), may hold values from 0 to 1, as said below
- rank_key: int32 [64], P('gal'), may hold values from 0 to 63, each once
Outputs:
- projector_basis: float32 [8192, 128], P('pix')
- scores: float32 [32768, 128], P('gal')
Inputs may be any that keep to these rules, and one draw needn't show every extreme that they name: `block_mask`: in every galaxy batch at least half of the 64 blocks are valid.
All inputs are finite; a program needn't handle non-finite values.
Results may differ from a plain program's by a relative error of at most 0.0059.
Values sent between devices are 32-bit elements; how exact they have to be, the bound alone decides.
No kernel may reach another device: no remote copies, remote signals or barrier semaphores. Data moves between devices by JAX's collectives and lax.ppermute only.
A program may use at most 64 MiB of HBM per device.

v0:
```python
import math
import jax
import jax.numpy as jnp
from jax import lax
from jax.sharding import PartitionSpec as P

NPIX = 8192
K = 128
ITERS = 2


def swapped(block, axis, bit):
    count = lax.axis_size(axis)
    route = []
    for low in range(count):
        high = low | 1 << bit
        if high != low and high < count:
            route += [(low, high), (high, low)]
    return lax.ppermute(block, axis, route)


def gram_of(left_side, right_side):
    return lax.dot_general(
        left_side,
        right_side,
        (((0,), (0,)), ((), ())),
        precision=lax.Precision.HIGHEST,
        preferred_element_type=jnp.float32,
    )


def matmul_high(left_side, right_side):
    return jnp.dot(
        left_side, right_side, precision=lax.Precision.HIGHEST, preferred_element_type=jnp.float32
    )


def orthonormal(columns, gram_matrix):
    lower_factor = jnp.linalg.cholesky(gram_matrix)
    return lax.linalg.triangular_solve(
        lower_factor, columns, left_side=False, lower=True, transpose_a=True
    )


def rotate(gram_matrix):
    rotation = jnp.concatenate(
        [jnp.eye(K, dtype=jnp.float32), jnp.zeros((K, K), jnp.float32)], axis=0
    )
    for iteration in range(ITERS):
        mapped = matmul_high(gram_matrix, rotation)
        rotation = orthonormal(mapped, gram_of(mapped, mapped))
    return rotation


def per_device(spectra, sketch, block_mask, rank_key):
    pixel_width = spectra.shape[1]
    pixel_mask = jnp.repeat(block_mask[0], pixel_width // block_mask.shape[1]).astype(jnp.bfloat16)
    masked = spectra * pixel_mask[None, :]
    sketched = lax.dot_general(
        masked, sketch, (((0,), (0,)), ((), ())), preferred_element_type=jnp.float32
    )
    gram_sum = lax.psum(gram_of(sketched, sketched), "pix")
    ortho_panel = orthonormal(sketched, gram_sum)
    ortho_half = ortho_panel.astype(jnp.bfloat16)
    projected = lax.psum(jnp.dot(masked, ortho_half, preferred_element_type=jnp.float32), "pix")
    covariance = gram_of(projected, projected)
    factor = jnp.linalg.cholesky(covariance)
    panel_now = matmul_high(ortho_panel, factor)
    own_gram = gram_of(factor, factor)
    all_keys = lax.all_gather(rank_key, "gal", axis=0, tiled=True)
    position = lax.axis_index("gal")
    level_count = lax.axis_size("gal").bit_length() - 1
    for section in range(level_count):
        block_span = 2**section
        group_min = jnp.min(all_keys.reshape(-1, block_span), axis=1)
        my_group = position // block_span
        own_min = group_min[my_group]
        other_min = group_min[jnp.bitwise_xor(my_group, 1)]
        lead_flag = own_min < other_min
        partner = swapped(panel_now, "gal", section)
        front_panel = jnp.where(lead_flag, panel_now, partner)
        back_panel = jnp.where(lead_flag, partner, panel_now)
        joined = jnp.concatenate([front_panel, back_panel], axis=1)
        gram_matrix = lax.psum(gram_of(joined, joined), "pix")
        rotation = rotate(gram_matrix)
        panel_now = matmul_high(joined, rotation)
        own_gram = gram_of(rotation, matmul_high(gram_matrix, rotation))
    projector_basis = orthonormal(panel_now, own_gram) * math.sqrt(NPIX)
    basis_half = projector_basis.astype(jnp.bfloat16)
    score_terms = jnp.dot(masked, basis_half, preferred_element_type=jnp.float32)
    scores = lax.psum(score_terms, "pix") / NPIX
    return (projector_basis, scores)


def solution(mesh):
    in_specs = (P("gal", "pix"), P("gal", None), P("gal", "pix"), P("gal"))
    out_specs = (P("pix", None), P("gal", None))
    return jax.shard_map(
        per_device, mesh=mesh, in_specs=in_specs, out_specs=out_specs, check_vma=False
    )
```

profile of v0, /device:TPU:2, one launch (start us, length us, event | category | flops | bytes accessed | tf_op | source)
XLA Modules:
  0.0 1212.3 jit_solution(16196803938518872094)
XLA Ops:
  11.5 81.2 %all-reduce.12.cloned.1.call-done = f32[128,128]{0,1:T(8,128)} async-done(((f32[128,128]{0,1:T(8,128)}), f32[128,128]{0,1:T(8,128)}) %all-reduce.12.cloned.1.call-update) | async-done | bytes 65552 | tf_op jit(solution)/shard_map/psum | solution.py:62
  94.5 11.7 cholesky.239
  119.5 76.4 %all-reduce.14.cloned.1.call-done = f32[512,128]{1,0:T(8,128)} async-done(((f32[512,128]{1,0:T(8,128)}), f32[512,128]{1,0:T(8,128)}) %all-reduce.14.cloned.1.call-update) | async-done | bytes 262160 | tf_op jit(solution)/shard_map/psum | solution.py:65
  197.6 11.7 cholesky.250
  215.9 20.6 %all-reduce.1 = s32[64]{0:T(128)S(1)} all-reduce(s32[64]{0:T(128)S(1)} %dynamic-update-slice.2), channel_id=1, replica_groups=mesh['gal'=64,'pix'=8] {'gal'}, use_global_device_ids=true, to_apply=%add.1 | all-reduce | flops 64 | bytes 512
  240.7 71.8 %all-reduce.16.cloned.1.call-done = f32[256,256]{1,0:T(8,128)} async-done(((f32[256,256]{1,0:T(8,128)}), f32[256,256]{1,0:T(8,128)}) %all-reduce.16.cloned.1.call-update) | async-done | bytes 262160 | tf_op jit(solution)/shard_map/psum | solution.py:84
  314.2 11.7 cholesky.261
  338.3 11.7 cholesky.272
  351.3 21.1 %custom-call.22 = f32[1,128,128]{1,2,0:T(8,128)S(1)} custom-call(f32[1,128,128]{2,1,0:T(8,128)S(1)} %fusion.38), custom_call_target="InvertDiagBlocksLowerTriangular" | custom-call | tf_op jit(solution)/shard_map/triangular_solve/custom-call.2 | solution.py:40
  386.4 76.7 %all-reduce.18.cloned.1.call-done = f32[256,256]{1,0:T(8,128)} async-done(((f32[256,256]{1,0:T(8,128)}), f32[256,256]{1,0:T(8,128)}) %all-reduce.18.cloned.1.call-update) | async-done | bytes 262160 | tf_op jit(solution)/shard_map/psum | solution.py:84
  464.9 11.7 cholesky.283
  489.0 11.7 cholesky.294
  520.0 16.3 %collective-permute-done.2 = f32[1024,128]{0,1:T(8,128)S(1)} collective-permute-done((f32[1024,128]{0,1:T(8,128)S(1)}, f32[1024,128]{0,1:T(8,128)S(1)}, u32[]{:S(2)}, u32[]{:S(2)}) %collective-permute-start.2) | collective-permute-done | bytes 524320 | tf_op jit(solution)/shard_map/ppermute | solution.py:19
  538.2 76.9 %all-reduce.20.cloned.1.call-done = f32[256,256]{1,0:T(8,128)} async-done(((f32[256,256]{1,0:T(8,128)}), f32[256,256]{1,0:T(8,128)}) %all-reduce.20.cloned.1.call-update) | async-done | bytes 262160 | tf_op jit(solution)/shard_map/psum | solution.py:84
  616.8 11.7 cholesky.305
  640.9 11.7 cholesky.316
  675.1 15.5 %collective-permute-done.3 = f32[1024,128]{0,1:T(8,128)S(1)} collective-permute-done((f32[1024,128]{0,1:T(8,128)S(1)}, f32[1024,128]{0,1:T(8,128)S(1)}, u32[]{:S(2)}, u32[]{:S(2)}) %collective-permute-start.3) | collective-permute-done | bytes 524320 | tf_op jit(solution)/shard_map/ppermute | solution.py:19
  692.5 77.3 %all-reduce.22.cloned.1.call-done = f32[256,256]{1,0:T(8,128)} async-done(((f32[256,256]{1,0:T(8,128)}), f32[256,256]{1,0:T(8,128)}) %all-reduce.22.cloned.1.call-update) | async-done | bytes 262160 | tf_op jit(solution)/shard_map/psum | solution.py:84
  771.5 11.7 cholesky.327
  795.6 11.7 cholesky.338
  832.9 76.7 %all-reduce.24.cloned.1.call-done = f32[256,256]{1,0:T(8,128)} async-done(((f32[256,256]{1,0:T(8,128)}), f32[256,256]{1,0:T(8,128)}) %all-reduce.24.cloned.1.call-update) | async-done | bytes 262160 | tf_op jit(solution)/shard_map/psum | solution.py:84
  911.3 11.7 cholesky.349
  973.9 76.7 %all-reduce.26.cloned.1.call-done = f32[256,256]{1,0:T(8,128)} async-done(((f32[256,256]{1,0:T(8,128)}), f32[256,256]{1,0:T(8,128)}) %all-reduce.26.cloned.1.call-update) | async-done | bytes 262160 | tf_op jit(solution)/shard_map/psum | solution.py:84
  1128.1 75.6 %all-reduce.28.cloned.1.call-done = f32[512,128]{1,0:T(8,128)} async-done(((f32[512,128]{1,0:T(8,128)}), f32[512,128]{1,0:T(8,128)}) %all-reduce.28.cloned.1.call-update) | async-done | bytes 262160 | tf_op jit(solution)/shard_map/psum | solution.py:91
  (223 shorter events, 296.8 us)
Async XLA Ops:
  7.2 0.9 copy-start
  7.2 85.5 %all-reduce.12.cloned.1.call-start = ((), (), s32[]{:S(2)}) async-start(), calls=%async_computation | async-start | bytes 131072 | tf_op jit(solution)/shard_map/psum | solution.py:62
  11.4 106.6 %copy-start.1 = (bf16[512,1024]{1,0:T(8,128)(2,1)S(1)}, bf16[512,1024]{1,0:T(8,128)(2,1)}, u32[]{:S(2)}) copy-start(bf16[512,1024]{1,0:T(8,128)(2,1)} %param.9) | copy-start | bytes 3145732
  11.4 184.4 %all-reduce.14.cloned.1.call-start = ((), (), s32[]{:S(2)}) async-start(), calls=%async_computation.1 | async-start | bytes 524288 | tf_op jit(solution)/shard_map/psum | solution.py:65
  119.2 193.3 %all-reduce.16.cloned.1.call-start = ((), (), s32[]{:S(2)}) async-start(), calls=%async_computation.2 | async-start | bytes 524288 | tf_op jit(solution)/shard_map/psum | solution.py:84
  211.3 27.1 %collective-permute-start = (f32[1024,128]{0,1:T(8,128)S(1)}, f32[1024,128]{0,1:T(8,128)S(1)}, u32[]{:S(2)}, u32[]{:S(2)}) collective-permute-start(f32[1024,128]{0,1:T(8,128)S(1)} %fusion.80), channel_id=1, source_target_pairs={{0,8},{8,0},{16,24},{24,16},{32,40},{40,32},{48,56},{56,48},{64,72... | collective-permute-start | bytes 1572872 | tf_op jit(solution)/shard_map/ppermute | solution.py:19
  240.3 222.9 %all-reduce.18.cloned.1.call-start = ((), (), s32[]{:S(2)}) async-start(), calls=%async_computation.3 | async-start | bytes 524288 | tf_op jit(solution)/shard_map/psum | solution.py:84
  325.9 11.5 copy-start.3
  373.5 11.1 collective-permute-start.1
  386.4 228.7 %all-reduce.20.cloned.1.call-start = ((), (), s32[]{:S(2)}) async-start(), calls=%async_computation.4 | async-start | bytes 524288 | tf_op jit(solution)/shard_map/psum | solution.py:84
  476.6 11.5 copy-start.4
  513.3 23.1 %collective-permute-start.2 = (f32[1024,128]{0,1:T(8,128)S(1)}, f32[1024,128]{0,1:T(8,128)S(1)}, u32[]{:S(2)}, u32[]{:S(2)}) collective-permute-start(f32[1024,128]{0,1:T(8,128)S(1)} %fusion.9), channel_id=1, source_target_pairs={{0,32},{32,0},{8,40},{40,8},{16,48},{48,16},{24,56},{56,24},{64,96... | collective-permute-start | bytes 1572872 | tf_op jit(solution)/shard_map/ppermute | solution.py:19
  538.2 231.6 %all-reduce.22.cloned.1.call-start = ((), (), s32[]{:S(2)}) async-start(), calls=%async_computation.5 | async-start | bytes 524288 | tf_op jit(solution)/shard_map/psum | solution.py:84
  628.6 11.5 copy-start.5
  665.0 25.6 %collective-permute-start.3 = (f32[1024,128]{0,1:T(8,128)S(1)}, f32[1024,128]{0,1:T(8,128)S(1)}, u32[]{:S(2)}, u32[]{:S(2)}) collective-permute-start(f32[1024,128]{0,1:T(8,128)S(1)} %fusion.7), channel_id=1, source_target_pairs={{0,64},{64,0},{8,72},{72,8},{16,80},{80,16},{24,88},{88,24},{32,96... | collective-permute-start | bytes 1572872 | tf_op jit(solution)/shard_map/ppermute | solution.py:19
  692.5 217.1 %all-reduce.24.cloned.1.call-start = ((), (), s32[]{:S(2)}) async-start(), calls=%async_computation.6 | async-start | bytes 524288 | tf_op jit(solution)/shard_map/psum | solution.py:84
  783.2 11.5 copy-start.6
  819.9 11.1 collective-permute-start.4
  832.8 217.9 %all-reduce.26.cloned.1.call-start = ((), (), s32[]{:S(2)}) async-start(), calls=%async_computation.7 | async-start | bytes 524288 | tf_op jit(solution)/shard_map/psum | solution.py:84
  923.0 11.5 copy-start.7
  959.4 12.6 %collective-permute-start.5 = (f32[1024,128]{0,1:T(8,128)S(1)}, f32[1024,128]{0,1:T(8,128)S(1)}, u32[]{:S(2)}, u32[]{:S(2)}) collective-permute-start(f32[1024,128]{0,1:T(8,128)S(1)} %fusion.3), channel_id=1, source_target_pairs={{0,256},{256,0},{8,264},{264,8},{16,272},{272,16},{24,280},{280,24... | collective-permute-start | bytes 1572872 | tf_op jit(solution)/shard_map/ppermute | solution.py:19
  973.9 229.8 %all-reduce.28.cloned.1.call-start = ((), (), s32[]{:S(2)}) async-start(), calls=%async_computation.8 | async-start | bytes 524288 | tf_op jit(solution)/shard_map/psum | solution.py:91
  1064.1 11.5 copy-start.2
Sparse Core Ops, SparseCore 0:
  11.6 81.1 all-reduce.11
  119.3 76.4 all-reduce.13
  240.4 71.9 all-reduce.15
  386.5 76.6 all-reduce.17
  538.3 76.7 all-reduce.19
  692.6 77.1 all-reduce.21
  832.9 76.6 all-reduce.23
  974.0 76.6 all-reduce.25
  1127.3 76.4 all-reduce.27
where the time goes:
time: 1220 us; the launch traced here: 1210 us
  waiting for transfers between devices  740 us (61%)
  other arithmetic  349 us (29%)
  matrix products  44 us (4%)
  starting transfers between devices  25.5 us (2%)
  between operations  23.8 us (2%)
  blocking collectives  20.6 us (2%)
    psum x6, waiting for transfers between devices, per_device(): gram_matrix = lax.psum(gram_of(joined, joined), 'pix')  456 us
    another operation x43, other arithmetic, orthonormal(): lower_factor = jnp.linalg.cholesky(gram_matrix)  173 us
    another operation x28, other arithmetic, orthonormal(): lax.linalg.triangular_solve(lower_factor, columns, left_side=False, lower...  159 us
    psum x1, waiting for transfers between devices, per_device(): gram_sum = lax.psum(gram_of(sketched, sketched), 'pix')  81.2 us
    psum x1, waiting for transfers between devices, per_device(): lax.psum(jnp.dot(masked, ortho_half, preferred_element_type=jnp.float32),...  76.4 us
    psum x1, waiting for transfers between devices, per_device(): scores = lax.psum(score_terms, 'pix') / NPIX  75.6 us
    ppermute x6, waiting for transfers between devices, swapped(): return lax.ppermute(block, axis, route)  50.1 us
    ppermute x6, starting transfers between devices, swapped(): return lax.ppermute(block, axis, route)  24.6 us
  transfers between devices with their start and end apart: 15, of which 14 were waited for; matrix products, arithmetic and copies ran while one was open for 1% of the time, Pallas kernels for 0%

commit v1 on v0

--- a/solution.py
+++ b/solution.py
@@ -81,7 +81,7 @@
         front_panel = jnp.where(lead_flag, panel_now, partner)
         back_panel = jnp.where(lead_flag, partner, panel_now)
         joined = jnp.concatenate([front_panel, back_panel], axis=1)
-        gram_matrix = lax.psum(gram_of(joined, joined), "pix")
+        gram_matrix = jnp.sum(lax.all_gather(gram_of(joined, joined), "pix"), axis=0)
         rotation = rotate(gram_matrix)
         panel_now = matmul_high(joined, rotation)
         own_gram = gram_of(rotation, matmul_high(gram_matrix, rotation))

time: 1220 us -> 1020 us (0.84)
  waiting for transfers between devices: 740 us -> 539 us
    psum x6 -> x0, waiting for transfers between devices: 456 us -> none  [per_device(): gram_matrix = lax.psum(gram_of(joined, joined), 'pix')]
    all_gather x0 -> x6, waiting for transfers between devices: none -> 250 us  [per_device(): lax.all_gather(gram_of(joined, joined), 'pix')]
where the time goes in v1:
time: 1020 us
  waiting for transfers between devices  539 us (53%)
  other arithmetic  360 us (35%)
  matrix products  38.4 us (4%)
  starting transfers between devices  25.5 us (2%)
  between operations  23.8 us (2%)
  blocking collectives  20.6 us (2%)
    all_gather x6, waiting for transfers between devices, per_device(): lax.all_gather(gram_of(joined, joined), 'pix')  250 us
    another operation x43, other arithmetic, orthonormal(): lower_factor = jnp.linalg.cholesky(gram_matrix)  173 us
    another operation x28, other arithmetic, orthonormal(): lax.linalg.triangular_solve(lower_factor, columns, left_side=False, lower...  159 us
    psum x1, waiting for transfers between devices, per_device(): gram_sum = lax.psum(gram_of(sketched, sketched), 'pix')  81.2 us
    psum x1, waiting for transfers between devices, per_device(): lax.psum(jnp.dot(masked, ortho_half, preferred_element_type=jnp.float32),...  76.4 us
    psum x1, waiting for transfers between devices, per_device(): scores = lax.psum(score_terms, 'pix') / NPIX  76 us
    ppermute x6, waiting for transfers between devices, swapped(): return lax.ppermute(block, axis, route)  54.8 us
    ppermute x6, starting transfers between devices, swapped(): return lax.ppermute(block, axis, route)  24.6 us
  transfers between devices with their start and end apart: 15, of which 14 were waited for; matrix products, arithmetic and copies ran while one was open for 1% of the time, Pallas kernels for 0%

profile of v1, /device:TPU:2, one launch (start us, length us, event | category | flops | bytes accessed | tf_op | source)
XLA Modules:
  0.0 1016.8 jit_solution(15229257849456385658)
XLA Ops:
  11.6 81.2 %all-reduce.6.cloned.1.call-done = f32[128,128]{0,1:T(8,128)} async-done(((f32[128,128]{0,1:T(8,128)}), f32[128,128]{0,1:T(8,128)}) %all-reduce.6.cloned.1.call-update) | async-done | bytes 65552 | tf_op jit(solution)/shard_map/psum | solution.py:62
  94.6 11.7 %cholesky.239 = f32[128,128]{1,0:T(8,128)S(1)} custom-call(f32[128,128]{1,0:T(8,128)S(1)} %fusion.78), custom_call_target="Cholesky" | custom-call | tf_op jit(solution)/shard_map/jit(cholesky)/cholesky | solution.py:39
  119.6 76.4 %all-reduce.8.cloned.1.call-done = f32[512,128]{1,0:T(8,128)} async-done(((f32[512,128]{1,0:T(8,128)}), f32[512,128]{1,0:T(8,128)}) %all-reduce.8.cloned.1.call-update) | async-done | bytes 262160 | tf_op jit(solution)/shard_map/psum | solution.py:65
  197.7 11.7 %cholesky.250 = f32[128,128]{1,0:T(8,128)S(1)} custom-call(f32[128,128]{1,0:T(8,128)S(1)} %fusion.76), custom_call_target="Cholesky" | custom-call | tf_op jit(solution)/shard_map/jit(cholesky)/cholesky | solution.py:67
  216.0 20.6 %all-reduce.1 = s32[64]{0:T(128)S(1)} all-reduce(s32[64]{0:T(128)S(1)} %dynamic-update-slice.2), channel_id=1, replica_groups=mesh['gal'=64,'pix'=8] {'gal'}, use_global_device_ids=true, to_apply=%add.1 | all-reduce | flops 64 | bytes 512
  240.8 37.6 %all-gather.13.cloned.1.call-done = f32[2048,256]{1,0:T(8,128)} async-done(((f32[256,256]{1,0:T(8,128)}), f32[2048,256]{1,0:T(8,128)}) %all-gather.13.cloned.1.call-update) | async-done | bytes 2097168 | tf_op jit(solution)/shard_map/all_gather | solution.py:84
  280.9 11.7 %cholesky.261 = f32[128,128]{1,0:T(8,128)S(1)} custom-call(f32[128,128]{1,0:T(8,128)S(1)} %fusion.75), custom_call_target="Cholesky" | custom-call | tf_op jit(solution)/shard_map/jit(cholesky)/cholesky | solution.py:39
  305.0 11.7 %cholesky.272 = f32[128,128]{1,0:T(8,128)S(1)} custom-call(f32[128,128]{1,0:T(8,128)S(1)} %fusion.73), custom_call_target="Cholesky" | custom-call | tf_op jit(solution)/shard_map/jit(cholesky)/cholesky | solution.py:39
  318.1 21.2 %custom-call.22 = f32[1,128,128]{1,2,0:T(8,128)S(1)} custom-call(f32[1,128,128]{2,1,0:T(8,128)S(1)} %fusion.38), custom_call_target="InvertDiagBlocksLowerTriangular" | custom-call | tf_op jit(solution)/shard_map/triangular_solve/custom-call.2 | solution.py:40
  354.1 42.5 %all-gather.15.cloned.1.call-done = f32[2048,256]{1,0:T(8,128)} async-done(((f32[256,256]{1,0:T(8,128)}), f32[2048,256]{1,0:T(8,128)}) %all-gather.15.cloned.1.call-update) | async-done | bytes 2097168 | tf_op jit(solution)/shard_map/all_gather | solution.py:84
  399.2 11.7 %cholesky.283 = f32[128,128]{1,0:T(8,128)S(1)} custom-call(f32[128,128]{1,0:T(8,128)S(1)} %fusion.71), custom_call_target="Cholesky" | custom-call | tf_op jit(solution)/shard_map/jit(cholesky)/cholesky | solution.py:39
  423.3 11.7 %cholesky.294 = f32[128,128]{1,0:T(8,128)S(1)} custom-call(f32[128,128]{1,0:T(8,128)S(1)} %fusion.69), custom_call_target="Cholesky" | custom-call | tf_op jit(solution)/shard_map/jit(cholesky)/cholesky | solution.py:39
  454.3 17.4 %collective-permute-done.2 = f32[1024,128]{0,1:T(8,128)S(1)} collective-permute-done((f32[1024,128]{0,1:T(8,128)S(1)}, f32[1024,128]{0,1:T(8,128)S(1)}, u32[]{:S(2)}, u32[]{:S(2)}) %collective-permute-start.2) | collective-permute-done | bytes 524320 | tf_op jit(solution)/shard_map/ppermute | solution.py:19
  473.6 42.4 %all-gather.17.cloned.1.call-done = f32[2048,256]{1,0:T(8,128)} async-done(((f32[256,256]{1,0:T(8,128)}), f32[2048,256]{1,0:T(8,128)}) %all-gather.17.cloned.1.call-update) | async-done | bytes 2097168 | tf_op jit(solution)/shard_map/all_gather | solution.py:84
  518.6 11.7 %cholesky.305 = f32[128,128]{1,0:T(8,128)S(1)} custom-call(f32[128,128]{1,0:T(8,128)S(1)} %fusion.67), custom_call_target="Cholesky" | custom-call | tf_op jit(solution)/shard_map/jit(cholesky)/cholesky | solution.py:39
  542.6 11.7 %cholesky.316 = f32[128,128]{1,0:T(8,128)S(1)} custom-call(f32[128,128]{1,0:T(8,128)S(1)} %fusion.65), custom_call_target="Cholesky" | custom-call | tf_op jit(solution)/shard_map/jit(cholesky)/cholesky | solution.py:39
  576.8 16.6 %collective-permute-done.3 = f32[1024,128]{0,1:T(8,128)S(1)} collective-permute-done((f32[1024,128]{0,1:T(8,128)S(1)}, f32[1024,128]{0,1:T(8,128)S(1)}, u32[]{:S(2)}, u32[]{:S(2)}) %collective-permute-start.3) | collective-permute-done | bytes 524320 | tf_op jit(solution)/shard_map/ppermute | solution.py:19
  595.3 42.8 %all-gather.19.cloned.1.call-done = f32[2048,256]{1,0:T(8,128)} async-done(((f32[256,256]{1,0:T(8,128)}), f32[2048,256]{1,0:T(8,128)}) %all-gather.19.cloned.1.call-update) | async-done | bytes 2097168 | tf_op jit(solution)/shard_map/all_gather | solution.py:84
  640.7 11.7 %cholesky.327 = f32[128,128]{1,0:T(8,128)S(1)} custom-call(f32[128,128]{1,0:T(8,128)S(1)} %fusion.63), custom_call_target="Cholesky" | custom-call | tf_op jit(solution)/shard_map/jit(cholesky)/cholesky | solution.py:39
  664.7 11.7 %cholesky.338 = f32[128,128]{1,0:T(8,128)S(1)} custom-call(f32[128,128]{1,0:T(8,128)S(1)} %fusion.61), custom_call_target="Cholesky" | custom-call | tf_op jit(solution)/shard_map/jit(cholesky)/cholesky | solution.py:39
  702.9 42.5 %all-gather.21.cloned.1.call-done = f32[2048,256]{1,0:T(8,128)} async-done(((f32[256,256]{1,0:T(8,128)}), f32[2048,256]{1,0:T(8,128)}) %all-gather.21.cloned.1.call-update) | async-done | bytes 2097168 | tf_op jit(solution)/shard_map/all_gather | solution.py:84
  747.9 11.7 %cholesky.349 = f32[128,128]{1,0:T(8,128)S(1)} custom-call(f32[128,128]{1,0:T(8,128)S(1)} %fusion.59), custom_call_target="Cholesky" | custom-call | tf_op jit(solution)/shard_map/jit(cholesky)/cholesky | solution.py:39
  811.4 42.5 %all-gather.23.cloned.1.call-done = f32[2048,256]{1,0:T(8,128)} async-done(((f32[256,256]{1,0:T(8,128)}), f32[2048,256]{1,0:T(8,128)}) %all-gather.23.cloned.1.call-update) | async-done | bytes 2097168 | tf_op jit(solution)/shard_map/all_gather | solution.py:84
  932.1 76.0 %all-reduce.10.cloned.1.call-done = f32[512,128]{1,0:T(8,128)} async-done(((f32[512,128]{1,0:T(8,128)}), f32[512,128]{1,0:T(8,128)}) %all-reduce.10.cloned.1.call-update) | async-done | bytes 262160 | tf_op jit(solution)/shard_map/psum | solution.py:91
  (217 shorter events, 304.3 us)
Async XLA Ops:
  7.2 0.9 copy-start
  7.2 85.6 %all-reduce.6.cloned.1.call-start = ((), (), s32[]{:S(2)}) async-start(), calls=%async_computation | async-start | bytes 131072 | tf_op jit(solution)/shard_map/psum | solution.py:62
  8.1 110.0 %copy-start.1 = (bf16[512,1024]{1,0:T(8,128)(2,1)S(1)}, bf16[512,1024]{1,0:T(8,128)(2,1)}, u32[]{:S(2)}) copy-start(bf16[512,1024]{1,0:T(8,128)(2,1)} %param.9) | copy-start | bytes 3145732
  11.5 184.4 %all-reduce.8.cloned.1.call-start = ((), (), s32[]{:S(2)}) async-start(), calls=%async_computation.1 | async-start | bytes 524288 | tf_op jit(solution)/shard_map/psum | solution.py:65
  119.3 159.1 %all-gather.13.cloned.1.call-start = ((), (), s32[]{:S(2)}) async-start(), calls=%async_computation.3 | async-start | bytes 2359296 | tf_op jit(solution)/shard_map/all_gather | solution.py:84
  211.3 27.1 %collective-permute-start = (f32[1024,128]{0,1:T(8,128)S(1)}, f32[1024,128]{0,1:T(8,128)S(1)}, u32[]{:S(2)}, u32[]{:S(2)}) collective-permute-start(f32[1024,128]{0,1:T(8,128)S(1)} %fusion.80), channel_id=1, source_target_pairs={{0,8},{8,0},{16,24},{24,16},{32,40},{40,32},{48,56},{56,48},{64,72... | collective-permute-start | bytes 1572872 | tf_op jit(solution)/shard_map/ppermute | solution.py:19
  240.4 156.3 %all-gather.15.cloned.1.call-start = ((), (), s32[]{:S(2)}) async-start(), calls=%async_computation.4 | async-start | bytes 2359296 | tf_op jit(solution)/shard_map/all_gather | solution.py:84
  340.3 11.9 %collective-permute-start.1 = (f32[1024,128]{0,1:T(8,128)S(1)}, f32[1024,128]{0,1:T(8,128)S(1)}, u32[]{:S(2)}, u32[]{:S(2)}) collective-permute-start(f32[1024,128]{0,1:T(8,128)S(1)} %fusion.11), channel_id=1, source_target_pairs={{0,16},{16,0},{8,24},{24,8},{32,48},{48,32},{40,56},{56,40},{64,80... | collective-permute-start | bytes 1572872 | tf_op jit(solution)/shard_map/ppermute | solution.py:19
  354.1 162.0 %all-gather.17.cloned.1.call-start = ((), (), s32[]{:S(2)}) async-start(), calls=%async_computation.5 | async-start | bytes 2359296 | tf_op jit(solution)/shard_map/all_gather | solution.py:84
  447.5 24.2 %collective-permute-start.2 = (f32[1024,128]{0,1:T(8,128)S(1)}, f32[1024,128]{0,1:T(8,128)S(1)}, u32[]{:S(2)}, u32[]{:S(2)}) collective-permute-start(f32[1024,128]{0,1:T(8,128)S(1)} %fusion.9), channel_id=1, source_target_pairs={{0,32},{32,0},{8,40},{40,8},{16,48},{48,16},{24,56},{56,24},{64,96... | collective-permute-start | bytes 1572872 | tf_op jit(solution)/shard_map/ppermute | solution.py:19
  473.6 164.6 %all-gather.19.cloned.1.call-start = ((), (), s32[]{:S(2)}) async-start(), calls=%async_computation.6 | async-start | bytes 2359296 | tf_op jit(solution)/shard_map/all_gather | solution.py:84
  566.7 26.7 %collective-permute-start.3 = (f32[1024,128]{0,1:T(8,128)S(1)}, f32[1024,128]{0,1:T(8,128)S(1)}, u32[]{:S(2)}, u32[]{:S(2)}) collective-permute-start(f32[1024,128]{0,1:T(8,128)S(1)} %fusion.7), channel_id=1, source_target_pairs={{0,64},{64,0},{8,72},{72,8},{16,80},{80,16},{24,88},{88,24},{32,96... | collective-permute-start | bytes 1572872 | tf_op jit(solution)/shard_map/ppermute | solution.py:19
  595.3 150.1 %all-gather.21.cloned.1.call-start = ((), (), s32[]{:S(2)}) async-start(), calls=%async_computation.7 | async-start | bytes 2359296 | tf_op jit(solution)/shard_map/all_gather | solution.py:84
  689.0 11.9 %collective-permute-start.4 = (f32[1024,128]{0,1:T(8,128)S(1)}, f32[1024,128]{0,1:T(8,128)S(1)}, u32[]{:S(2)}, u32[]{:S(2)}) collective-permute-start(f32[1024,128]{0,1:T(8,128)S(1)} %fusion.5), channel_id=1, source_target_pairs={{0,128},{128,0},{8,136},{136,8},{16,144},{144,16},{24,152},{152,24... | collective-permute-start | bytes 1572872 | tf_op jit(solution)/shard_map/ppermute | solution.py:19
  702.8 151.1 %all-gather.23.cloned.1.call-start = ((), (), s32[]{:S(2)}) async-start(), calls=%async_computation.8 | async-start | bytes 2359296 | tf_op jit(solution)/shard_map/all_gather | solution.py:84
  796.0 13.4 %collective-permute-start.5 = (f32[1024,128]{0,1:T(8,128)S(1)}, f32[1024,128]{0,1:T(8,128)S(1)}, u32[]{:S(2)}, u32[]{:S(2)}) collective-permute-start(f32[1024,128]{0,1:T(8,128)S(1)} %fusion.3), channel_id=1, source_target_pairs={{0,256},{256,0},{8,264},{264,8},{16,272},{272,16},{24,280},{280,24... | collective-permute-start | bytes 1572872 | tf_op jit(solution)/shard_map/ppermute | solution.py:19
  811.3 196.8 %all-reduce.10.cloned.1.call-start = ((), (), s32[]{:S(2)}) async-start(), calls=%async_computation.2 | async-start | bytes 524288 | tf_op jit(solution)/shard_map/psum | solution.py:91
Sparse Core Ops, SparseCore 0:
  11.6 81.1 all-reduce.5
  119.4 76.4 all-reduce.7
  240.5 37.8 all-gather.12
  354.2 42.4 all-gather.14
  473.7 42.3 all-gather.16
  595.4 42.7 all-gather.18
  702.9 42.4 all-gather.20
  811.5 42.4 all-gather.22
  931.3 76.8 all-reduce.9
